TPU v7x, 32 devices: a whole 2x2x4 slice. The times are simulated.
32 devices in a mesh: job: 2 (over y), cuts: 4 (over x, core), mesh: 4 (over z).
Axes of the slice: x: 2, y: 2, z: 4, core: 2. Of those that a mesh axis runs over, the one named last changes fastest.
Arguments:
- blocks: bfloat16 [512, 12288], P(('job', 'cuts'), 'mesh'), parts along dimension 0, may hold values from -6 to 6
- boundary_shift: int32 [8], P(('job', 'cuts')), parts along dimension 0, may hold values from -32 to 32, as said below
- centre: float32 [8], P(('job', 'cuts')), parts along dimension 0, may hold values from -1 to 1
- half_width: float32 [8], P(('job', 'cuts')), parts along dimension 0, may hold values from 1 to 2
- cell_matrix: bfloat16 [216, 216], replicated, may hold values from -0.4375 to 0.4375
- cell_coef: float32 [256], P(('job', 'mesh')), parts along dimension 0, may hold values from 0.3 to 1.5
- connectivity: int32 [216, 256], P(None, ('job', 'mesh')), parts along dimension 1, may hold values from 0 to 3327
- halo_list: int32 [2048], P(('job', 'mesh')), parts along dimension 0, may hold values from 0 to 3071, as said below
- mass: float32 [24576], P(('job', 'mesh')), parts along dimension 0, may hold values from 0.5 to 3.6
- potential: float32 [24576], P(('job', 'mesh')), parts along dimension 0, may hold values from 0.2 to 1
Outputs:
- filtered: float32 [512, 12288], P(('job', 'cuts'), 'mesh'), parts along dimension 0
There are 2 independent parts, one for each index of `job`. A program takes and returns all parts, laid end to end along the dimension named above; an argument that names none is the same for every part. Nothing has to cross between parts.
Inputs may be any that keep to these rules, and one draw needn't show every extreme that they name: `boundary_shift`: every entry lies within 32 in size; the first slice's is not negative and the last slice's not positive; both ends of the range are reached. `halo_list`: the 256 entries of each device's list are distinct owned nodes, and each list holds 0 and 3071.
All inputs are finite; a program needn't handle non-finite values.
Results may differ from a plain program's by a relative error of at most 0.0028.
Values may be sent and summed in bfloat16 or wider, within the bound.
A program may use at most 64 MiB of HBM per device.

v0:
```python
import jax
import jax.numpy as jnp
from jax import lax
from jax.sharding import PartitionSpec as P


def passed_along(array, axis, by):
    count = lax.axis_size(axis)
    pairs = [(i, i + by) for i in range(count) if 0 <= i + by < count]
    return lax.ppermute(array, axis, pairs)


def extended_2(array, sides, width):
    for axis, dim in sides:
        count, length = (lax.axis_size(axis), array.shape[dim])
        up = [(i, (i + 1) % count) for i in range(count - 1)]
        down = [(j, i) for i, j in up]
        last = lax.slice_in_dim(array, length - width, length, axis=dim)
        leading = lax.slice_in_dim(array, 0, width, axis=dim)
        before = lax.ppermute(last, axis, up)
        after = lax.ppermute(leading, axis, down)
        array = jnp.concatenate([before, array, after], axis=dim)
    return array


def apply_operator(vec, connectivity, halo_list, cell_matrix, cell_coef, mass, potential):
    owned_count = vec.shape[1]
    send_rows = jnp.take(vec, halo_list, axis=1)
    ghost = passed_along(send_rows, "mesh", -1)
    local_rows = jnp.concatenate([vec, ghost], axis=1)
    values = jnp.take(local_rows, connectivity, axis=1)
    products = (
        jnp.einsum("ij,vjc->vic", cell_matrix, values, preferred_element_type=jnp.float32)
        * cell_coef
    )
    summed = (
        jnp.zeros((vec.shape[0], local_rows.shape[1]), jnp.float32)
        .at[:, connectivity]
        .add(products)
    )
    returned = passed_along(summed[:, owned_count:], "mesh", 1)
    owned = summed[:, :owned_count].at[:, halo_list].add(returned)
    return owned / mass + potential * vec.astype(jnp.float32)


def body(
    blocks,
    boundary_shift,
    centre,
    half_width,
    cell_matrix,
    cell_coef,
    connectivity,
    halo_list,
    mass,
    potential,
):
    rows = blocks.shape[0]
    extended = extended_2(blocks, (("cuts", 0),), rows)
    window = lax.dynamic_slice_in_dim(extended, rows + boundary_shift[0], rows, 0)
    middle = centre[0]
    spread = half_width[0]
    first = (
        (
            apply_operator(window, connectivity, halo_list, cell_matrix, cell_coef, mass, potential)
            - middle * window.astype(jnp.float32)
        )
        / spread
    ).astype(jnp.bfloat16)
    second = 2.0 * (
        apply_operator(first, connectivity, halo_list, cell_matrix, cell_coef, mass, potential)
        - middle * first.astype(jnp.float32)
    ) / spread - window.astype(jnp.float32)
    node_count = blocks.shape[1] * lax.axis_size("mesh")
    partial_gram = jnp.dot(second * mass, second.T, precision=lax.Precision.HIGHEST) / node_count
    gram = lax.psum(partial_gram, "mesh")
    lower = jnp.linalg.cholesky(gram)
    return lax.linalg.triangular_solve(lower, second, left_side=True, lower=True)


def solution(mesh):
    return jax.shard_map(
        body,
        mesh=mesh,
        in_specs=(
            P(("job", "cuts"), "mesh"),
            P(("job", "cuts")),
            P(("job", "cuts")),
            P(("job", "cuts")),
            P(),
            P(("job", "mesh")),
            P(None, ("job", "mesh")),
            P(("job", "mesh")),
            P(("job", "mesh")),
            P(("job", "mesh")),
        ),
        out_specs=P(("job", "cuts"), "mesh"),
        check_vma=False,
    )
```

profile of v0, /device:TPU:2, one launch (start us, length us, event | category | flops | bytes accessed | tf_op | source)
XLA Modules:
  0.0 214.1 jit_solution(16234078214406584874)
XLA Ops:
  0.0 2.0 collective-permute-start
  2.1 3.6 %collective-permute-start.1 = (bf16[64,3072]{1,0:T(8,128)(2,1)}, bf16[64,3072]{1,0:T(8,128)(2,1)S(1)}, u32[]{:S(2)}, u32[]{:S(2)}) collective-permute-start(bf16[64,3072]{1,0:T(8,128)(2,1)} %param.14), channel_id=1, source_target_pairs={{4,0},{8,4},{12,8},{5,1},{9,5},{13,9},{6,2},{10,6},{14,10},{7,3},{... | collective-permute-start | bytes 1179656 | tf_op jit(solution)/shard_map/ppermute | solution.py:21
  5.7 0.7 compare_select_fusion.1
  6.4 0.8 compare_select_fusion
  7.2 0.7 compare_and_fusion.1
  7.8 1.4 copy.32
  9.9 0.1 copy.30
  10.0 0.1 reshape.76
  10.2 0.4 copy.31
  10.5 0.8 collective-permute-done.1
  11.3 0.4 copy.33
  11.7 1.2 fusion.24
  12.9 0.9 gather_fusion
  13.8 0.1 select_bitcast_fusion.1
  13.9 1.3 collective-permute-start.2
  15.2 4.8 %collective-permute-done.2 = bf16[64,256]{0,1:T(8,128)(2,1)S(1)} collective-permute-done((bf16[64,256]{0,1:T(8,128)(2,1)S(1)}, bf16[64,256]{0,1:T(8,128)(2,1)S(1)}, u32[]{:S(2)}, u32[]{:S(2)}) %collective-permute-start.2) | collective-permute-done | bytes 32800 | tf_op jit(solution)/shard_map/ppermute | solution.py:10
  20.1 0.2 pad_maximum_fusion
  20.2 13.0 %gather_fusion.1 = bf16[6912,64]{1,0:T(8,128)(2,1)S(1)} fusion(bf16[64,3328]{0,1:T(8,128)(2,1)S(1)} %pad_maximum_fusion, s32[7168]{0:T(1024)S(1)} %pad_clamp_fusion), kind=kCustom, calls=%fused_computation.1.clone | custom fusion | bytes 1797120 | tf_op jit(solution)/shard_map/jit(_take)/gather | solution.py:31
  33.3 3.3 %copy.35 = bf16[216,32,64]{0,1,2:T(8,128)(2,1)} copy(bf16[216,32,64]{2,1,0:T(8,128)(2,1)S(1)} %bitcast.49) | data formatting | bytes 1769472 | tf_op jit(solution)/shard_map/jit(_take)/gather | solution.py:31
  36.6 1.7 multiply_bitcast_fusion.1
  38.3 3.6 %copy.36 = f32[216,32,64]{2,1,0:T(8,128)} copy(f32[216,32,64]{0,1,2:T(8,128)S(1)} %multiply_bitcast_fusion.1) | data formatting | bytes 3538944 | tf_op jit(solution)/shard_map/mul | solution.py:33
  41.9 39.4 %scatter_custom_fusion = f32[64,3328]{0,1:T(8,128)S(1)} fusion(s32[6912]{0:T(1024)} %copy-done.4, f32[6912,64]{1,0:T(8,128)} %bitcast.51, f32[]{:T(128)} %constant.71.clone.1), kind=kCustom, calls=%fused_computation.39 | custom fusion | flops 442368 | bytes 852480 | tf_op jit(solution)/shard_map/scatter-add | solution.py:39
  81.4 3.5 %collective-permute-start.3 = (f32[64,256]{0,1:T(8,128)S(1)}, f32[64,256]{0,1:T(8,128)S(1)}, u32[]{:S(2)}, u32[]{:S(2)}) collective-permute-start(f32[64,256]{0,1:T(8,128)S(1)} %slice.35), channel_id=1, source_target_pairs={{0,1},{1,2},{2,3},{4,5},{5,6},{6,7},{8,9},{9,10},{10,11},{12,13},{... | collective-permute-start | bytes 196616 | tf_op jit(solution)/shard_map/ppermute | solution.py:10
  86.2 1.3 slice.34
  87.5 4.5 %scatter_custom_fusion.1 = f32[64,3072]{0,1:T(8,128)} fusion(f32[64,3072]{0,1:T(8,128)} %slice.34, s32[256]{0:T(256)} %copy-done.10, f32[64,256]{0,1:T(8,128)S(1)} %collective-permute-done.3), kind=kCustom, calls=%fused_computation.48 | custom fusion | flops 16384 | bytes 851968 | tf_op jit(solution)/shard_map/scatter-add | solution.py:42
  92.0 2.8 %fusion.9 = bf16[64,3072]{0,1:T(8,128)(2,1)S(1)} fusion(bf16[64,3072]{0,1:T(8,128)(2,1)S(1)} %fusion.24, f32[64,3072]{0,1:T(8,128)} %scatter_custom_fusion.1, f32[]{:T(128)} %bitcast.46, f32[]{:T(128)} %bitcast.44, f32[3072]{0:T(1024)S(1)} %copy-done.7, f32[3072]{0:T(1024)S(1)} %copy-done.5), kind=kLoop, calls=%fused_computation.27 | loop fusion | flops 1572864 | bytes 1597448 | tf_op jit(solution)/shard_map/convert_element_type | solution.py:69
  94.8 1.0 gather_fusion.2
  95.8 0.1 select_bitcast_fusion
  95.9 1.5 collective-permute-start.4
  97.4 5.0 %collective-permute-done.4 = bf16[64,256]{0,1:T(8,128)(2,1)S(1)} collective-permute-done((bf16[64,256]{0,1:T(8,128)(2,1)S(1)}, bf16[64,256]{0,1:T(8,128)(2,1)S(1)}, u32[]{:S(2)}, u32[]{:S(2)}) %collective-permute-start.4) | collective-permute-done | bytes 32800 | tf_op jit(solution)/shard_map/ppermute | solution.py:10
  102.4 0.2 pad_maximum_fusion.1
  102.6 13.0 %gather_fusion.3 = bf16[6912,64]{1,0:T(8,128)(2,1)S(1)} fusion(bf16[64,3328]{0,1:T(8,128)(2,1)S(1)} %pad_maximum_fusion.1, s32[7168]{0:T(1024)S(1)} %pad_clamp_fusion), kind=kCustom, calls=%fused_computation.3.clone | custom fusion | bytes 1797120 | tf_op jit(solution)/shard_map/jit(_take)/gather | solution.py:31
  115.7 3.3 %copy.38 = bf16[216,32,64]{0,1,2:T(8,128)(2,1)} copy(bf16[216,32,64]{2,1,0:T(8,128)(2,1)S(1)} %bitcast.48) | data formatting | bytes 1769472 | tf_op jit(solution)/shard_map/jit(_take)/gather | solution.py:31
  119.0 1.7 multiply_bitcast_fusion
  120.7 3.6 %copy.39 = f32[216,32,64]{2,1,0:T(8,128)} copy(f32[216,32,64]{0,1,2:T(8,128)S(1)} %multiply_bitcast_fusion) | data formatting | bytes 3538944 | tf_op jit(solution)/shard_map/mul | solution.py:33
  124.3 39.4 %scatter_custom_fusion.2 = f32[64,3328]{0,1:T(8,128)S(1)} fusion(s32[6912]{0:T(1024)} %copy-done.4, f32[6912,64]{1,0:T(8,128)} %bitcast.50, f32[]{:T(128)} %constant.71.clone.1), kind=kCustom, calls=%fused_computation.37 | custom fusion | flops 442368 | bytes 852480 | tf_op jit(solution)/shard_map/scatter-add | solution.py:39
  163.8 3.9 %collective-permute-start.5 = (f32[64,256]{0,1:T(8,128)S(1)}, f32[64,256]{0,1:T(8,128)S(1)}, u32[]{:S(2)}, u32[]{:S(2)}) collective-permute-start(f32[64,256]{0,1:T(8,128)S(1)} %slice.37), channel_id=1, source_target_pairs={{0,1},{1,2},{2,3},{4,5},{5,6},{6,7},{8,9},{9,10},{10,11},{12,13},{... | collective-permute-start | bytes 196616 | tf_op jit(solution)/shard_map/ppermute | solution.py:10
  167.7 1.3 slice.36
  169.0 1.2 collective-permute-done.5
  170.2 4.5 %scatter_custom_fusion.3 = f32[64,3072]{0,1:T(8,128)} fusion(f32[64,3072]{0,1:T(8,128)} %slice.36, s32[256]{0:T(256)} %copy-done.10, f32[64,256]{0,1:T(8,128)S(1)} %collective-permute-done.5), kind=kCustom, calls=%fused_computation.46 | custom fusion | flops 16384 | bytes 851968 | tf_op jit(solution)/shard_map/scatter-add | solution.py:42
  174.7 2.8 %convert_subtract_fusion = f32[64,3072]{0,1:T(8,128)S(1)} fusion(bf16[64,3072]{0,1:T(8,128)(2,1)S(1)} %fusion.24, bf16[64,3072]{0,1:T(8,128)(2,1)S(1)} %copy-done.2, f32[64,3072]{0,1:T(8,128)} %scatter_custom_fusion.3, f32[]{:T(128)} %bitcast.47, f32[]{:T(128)} %bitcast.45, f32[3072]{0:T(1024)S(1)} %copy-done.8, f32[3072]{0:T(1024)S(1)} %copy-done.6), kind=kLoop, calls=%fused_computation.10 | loop fusion | flops 1966080 | bytes 2383880 | tf_op jit(solution)/shard_map/sub | solution.py:70
  177.5 3.2 %fusion.10 = f32[64,64]{0,1:T(8,128)S(1)} fusion(f32[64,3072]{0,1:T(8,128)S(1)} %convert_subtract_fusion, f32[3072]{0:T(1024)S(1)} %copy-done.6), kind=kOutput, calls=%fused_computation.28 | convolution fusion | flops 151195648 | bytes 815104 | tf_op jit(solution)/shard_map/dot_general | solution.py:75
  180.7 18.6 %psum.7 = f32[64,64]{0,1:T(8,128)S(1)} all-reduce(f32[64,64]{0,1:T(8,128)S(1)} %fusion.10), channel_id=1, replica_groups=mesh['job'=2,'cuts'=4,'mesh'=4] {'mesh'}, use_global_device_ids=true, to_apply=%region_4.7 | all-reduce | flops 4096 | bytes 32768 | tf_op jit(solution)/shard_map/psum | solution.py:76
  199.3 5.8 %cholesky.16 = f32[64,64]{1,0:T(8,128)S(1)} custom-call(f32[64,64]{1,0:T(8,128)S(1)} %fusion.37), custom_call_target="Cholesky" | custom-call | tf_op jit(solution)/shard_map/jit(cholesky)/cholesky | solution.py:77
  205.2 0.6 compare_reduce_fusion
  205.8 0.7 fusion.34
  206.5 4.9 %custom-call.6 = f32[1,64,64]{1,2,0:T(8,128)S(1)} custom-call(f32[1,64,64]{2,1,0:T(8,128)S(1)} %fusion.34), custom_call_target="InvertDiagBlocksLowerTriangular" | custom-call | tf_op jit(solution)/shard_map/triangular_solve | solution.py:78
  211.4 2.7 %fusion.35 = f32[64,3072]{1,0:T(8,128)} fusion(f32[64,3072]{0,1:T(8,128)S(1)} %convert_subtract_fusion, f32[1,64,64]{1,2,0:T(8,128)S(1)} %custom-call.6), kind=kOutput, calls=%fused_computation.57 | convolution fusion | flops 150994944 | bytes 1589248 | tf_op jit(solution)/shard_map/triangular_solve | solution.py:78
  (40 shorter events, 0.2 us)
Async XLA Ops:
  0.0 36.6 %copy-start = (bf16[216,216]{1,0:T(8,128)(2,1)S(1)}, bf16[216,216]{1,0:T(8,128)(2,1)}, u32[]{:S(2)}) copy-start(bf16[216,216]{1,0:T(8,128)(2,1)} %param.18) | copy-start | bytes 279940
  0.0 10.1 %copy-start.3 = (s32[216,32]{0,1:T(8,128)S(1)}, s32[216,32]{0,1:T(8,128)}, u32[]{:S(2)}) copy-start(s32[216,32]{0,1:T(8,128)} %param.20) | copy-start | bytes 82948
  0.0 10.1 %collective-permute-start = (bf16[64,3072]{1,0:T(8,128)(2,1)}, bf16[64,3072]{1,0:T(8,128)(2,1)S(1)}, u32[]{:S(2)}, u32[]{:S(2)}) collective-permute-start(bf16[64,3072]{1,0:T(8,128)(2,1)} %param.14), channel_id=1, source_target_pairs={{0,4},{4,8},{8,12},{1,5},{5,9},{9,13},{2,6},{6,10},{10,14},{3,7},{... | collective-permute-start | bytes 1179656 | tf_op jit(solution)/shard_map/ppermute | solution.py:20
  2.1 9.2 %collective-permute-start.1 = (bf16[64,3072]{1,0:T(8,128)(2,1)}, bf16[64,3072]{1,0:T(8,128)(2,1)S(1)}, u32[]{:S(2)}, u32[]{:S(2)}) collective-permute-start(bf16[64,3072]{1,0:T(8,128)(2,1)} %param.14), channel_id=1, source_target_pairs={{4,0},{8,4},{12,8},{5,1},{9,5},{13,9},{6,2},{10,6},{14,10},{7,3},{... | collective-permute-start | bytes 1179656 | tf_op jit(solution)/shard_map/ppermute | solution.py:21
  6.4 4.9 %copy-start.10 = (s32[256]{0:T(256)}, s32[256]{0:T(256)S(1)}, u32[]{:S(2)}) copy-start(s32[256]{0:T(256)S(1)} %compare_select_fusion.1) | copy-start | bytes 3076
  7.8 5.9 %copy-start.11 = (pred[256]{0:T(512)(128)(4,1)}, pred[256]{0:T(512)(128)(4,1)S(1)}, u32[]{:S(2)}) copy-start(pred[256]{0:T(512)(128)(4,1)S(1)} %compare_and_fusion.1) | copy-start | bytes 772
  10.1 5.1 %copy-start.4 = (s32[6912]{0:T(1024)}, s32[6912]{0:T(1024)S(1)}, u32[]{:S(2)}) copy-start(s32[6912]{0:T(1024)S(1)} %reshape.76) | copy-start | bytes 82948
  10.1 2.8 %copy-start.9 = (s32[1024]{0:T(1024)}, s32[1024]{0:T(1024)S(1)}, u32[]{:S(2)}) copy-start(s32[1024]{0:T(1024)S(1)} %pad_clamp_fusion.1) | copy-start | bytes 12292
  13.9 6.2 %collective-permute-start.2 = (bf16[64,256]{0,1:T(8,128)(2,1)S(1)}, bf16[64,256]{0,1:T(8,128)(2,1)S(1)}, u32[]{:S(2)}, u32[]{:S(2)}) collective-permute-start(bf16[64,256]{0,1:T(8,128)(2,1)S(1)} %select_bitcast_fusion.1), channel_id=1, source_target_pairs={{1,0},{2,1},{3,2},{5,4},{6,5},{7,6},{9,8},{10,9},{11,10},{13,12},{... | collective-permute-start | bytes 98312 | tf_op jit(solution)/shard_map/ppermute | solution.py:10
  33.3 3.3 %copy-start.13 = (f32[32]{0:T(128)S(1)}, f32[32]{0:T(128)}, u32[]{:S(2)}) copy-start(f32[32]{0:T(128)} %param.19) | copy-start | bytes 388
  81.4 6.1 %collective-permute-start.3 = (f32[64,256]{0,1:T(8,128)S(1)}, f32[64,256]{0,1:T(8,128)S(1)}, u32[]{:S(2)}, u32[]{:S(2)}) collective-permute-start(f32[64,256]{0,1:T(8,128)S(1)} %slice.35), channel_id=1, source_target_pairs={{0,1},{1,2},{2,3},{4,5},{5,6},{6,7},{8,9},{9,10},{10,11},{12,13},{... | collective-permute-start | bytes 196616 | tf_op jit(solution)/shard_map/ppermute | solution.py:10
  87.5 4.5 %copy-start.5 = (f32[3072]{0:T(1024)S(1)}, f32[3072]{0:T(1024)}, u32[]{:S(2)}) copy-start(f32[3072]{0:T(1024)} %param.22) | copy-start | bytes 36868
  87.5 4.5 %copy-start.7 = (f32[3072]{0:T(1024)S(1)}, f32[3072]{0:T(1024)}, u32[]{:S(2)}) copy-start(f32[3072]{0:T(1024)} %param.23) | copy-start | bytes 36868
  92.0 3.8 %copy-start.12 = (pred[256]{0:T(512)(128)(4,1)S(1)}, pred[256]{0:T(512)(128)(4,1)}, u32[]{:S(2)}) copy-start(pred[256]{0:T(512)(128)(4,1)} %copy-done.11) | copy-start | bytes 772
  94.8 7.6 %copy-start.1 = (bf16[64,3072]{0,1:T(8,128)(2,1)}, bf16[64,3072]{0,1:T(8,128)(2,1)S(1)}, u32[]{:S(2)}) copy-start(bf16[64,3072]{0,1:T(8,128)(2,1)S(1)} %fusion.9) | copy-start | bytes 1179652
  95.9 6.5 %collective-permute-start.4 = (bf16[64,256]{0,1:T(8,128)(2,1)S(1)}, bf16[64,256]{0,1:T(8,128)(2,1)S(1)}, u32[]{:S(2)}, u32[]{:S(2)}) collective-permute-start(bf16[64,256]{0,1:T(8,128)(2,1)S(1)} %select_bitcast_fusion), channel_id=1, source_target_pairs={{1,0},{2,1},{3,2},{5,4},{6,5},{7,6},{9,8},{10,9},{11,10},{13,12},{... | collective-permute-start | bytes 98312 | tf_op jit(solution)/shard_map/ppermute | solution.py:10
  115.6 3.3 %copy-start.14 = (f32[32]{0:T(128)S(1)}, f32[32]{0:T(128)}, u32[]{:S(2)}) copy-start(f32[32]{0:T(128)} %param.19) | copy-start | bytes 388
  163.8 6.4 %collective-permute-start.5 = (f32[64,256]{0,1:T(8,128)S(1)}, f32[64,256]{0,1:T(8,128)S(1)}, u32[]{:S(2)}, u32[]{:S(2)}) collective-permute-start(f32[64,256]{0,1:T(8,128)S(1)} %slice.37), channel_id=1, source_target_pairs={{0,1},{1,2},{2,3},{4,5},{5,6},{6,7},{8,9},{9,10},{10,11},{12,13},{... | collective-permute-start | bytes 196616 | tf_op jit(solution)/shard_map/ppermute | solution.py:10
  169.0 5.7 %copy-start.2 = (bf16[64,3072]{0,1:T(8,128)(2,1)S(1)}, bf16[64,3072]{0,1:T(8,128)(2,1)}, u32[]{:S(2)}) copy-start(bf16[64,3072]{0,1:T(8,128)(2,1)} %copy-done.1) | copy-start | bytes 1179652
  169.0 5.7 %copy-start.6 = (f32[3072]{0:T(1024)S(1)}, f32[3072]{0:T(1024)}, u32[]{:S(2)}) copy-start(f32[3072]{0:T(1024)} %param.22) | copy-start | bytes 36868
  169.0 5.7 %copy-start.8 = (f32[3072]{0:T(1024)S(1)}, f32[3072]{0:T(1024)}, u32[]{:S(2)}) copy-start(f32[3072]{0:T(1024)} %param.23) | copy-start | bytes 36868
where the time goes:
time: 215 us; the launch traced here: 214 us
  other arithmetic  109 us (51%)
  local copies, waits for them, and re-layouts  46.8 us (22%)
  blocking collectives  18.6 us (9%)
  starting transfers between devices  15.9 us (7%)
  waiting for transfers between devices  11.8 us (5%)
  matrix products  9.24 us (4%)
  between operations  2.29 us (1%)
    scatter-add x2, other arithmetic, apply_operator(): summed = jnp.zeros((vec.shape[0], local_rows.shape[1]), jnp.float32).at[:...  78.9 us
    gather x4, local copies, waits for them, and re-layouts, apply_operator(): values = jnp.take(local_rows, connectivity, axis=1)  32.7 us
    psum x1, blocking collectives, body(): gram = lax.psum(partial_gram, 'mesh')  18.6 us
    ppermute x4, waiting for transfers between devices, passed_along(): return lax.ppermute(array, axis, pairs)  11.1 us
    ppermute x4, starting transfers between devices, passed_along(): return lax.ppermute(array, axis, pairs)  10.2 us
    scatter-add x2, other arithmetic, apply_operator(): owned = summed[:, :owned_count].at[:, halo_list].add(returned)  8.96 us
    mul x2, local copies, waits for them, and re-layouts, apply_operator(): jnp.einsum('ij,vjc->vic', cell_matrix, values, preferred_element_type=jnp...  7.25 us
    another operation x3, other arithmetic, body(): lower = jnp.linalg.cholesky(gram)  6.52 us
  transfers between devices with their start and end apart: 6, of which 4 were waited for; matrix products, arithmetic and copies ran while one was open for 3% of the time, Pallas kernels for 0%

commit v1 on v0

v1 whole, which is shorter than its diff:
```python
import functools
import jax
import jax.numpy as jnp
from jax import lax
from jax.experimental import pallas as pl
from jax.experimental.pallas import tpu as pltpu
from jax.sharding import PartitionSpec as P

MESH = pl.DeviceIdType.MESH
F32, BF16 = jnp.float32, jnp.bfloat16
W = 256
UNROLL = 4
NT = (((1,), (1,)), ((), ()))
NN = (((1,), (0,)), ((), ()))


def dot(a, b, dims=NN, precision=None):
    return lax.dot_general(a, b, dims, precision=precision, preferred_element_type=F32)


def kernel(
    n_cuts, n_mesh,
    blocks, shift, centre, half_width, cell_matrix, coef, conn, halo, mass, potential,
    out,
    ext, win, fst, onehot, idx, group, kpad, acc, masked, ghost_out, ret, second, grams,
    cut_send, cut_recv, ghost_send, ghost_recv, ret_send, ret_recv, gram_send, gram_recv,
):
    rows, nodes = blocks.shape
    half = rows // 2
    cells = conn.shape[1]
    owned = nodes // W
    parts = owned + 1
    cut, me = lax.axis_index("cuts"), lax.axis_index("mesh")

    barrier = pltpu.get_barrier_semaphore()

    @pl.when(cut > 0)
    def _():
        pl.semaphore_signal(barrier, inc=1, device_id={"cuts": cut - 1}, device_id_type=MESH)

    @pl.when(cut < n_cuts - 1)
    def _():
        pl.semaphore_signal(barrier, inc=1, device_id={"cuts": cut + 1}, device_id_type=MESH)

    for step in range(1, n_mesh):
        pl.semaphore_signal(
            barrier, inc=1, device_id={"mesh": lax.rem(me + step, n_mesh)}, device_id_type=MESH
        )
    greeted = (n_mesh - 1) + jnp.where(cut > 0, 1, 0) + jnp.where(cut < n_cuts - 1, 1, 0)
    pl.semaphore_wait(barrier, greeted)

    def edge(up):
        return pltpu.make_async_remote_copy(
            src_ref=blocks.at[pl.ds(half if up else 0, half)],
            dst_ref=ext.at[pl.ds(0 if up else half + rows, half)],
            send_sem=cut_send.at[0 if up else 1],
            recv_sem=cut_recv.at[0 if up else 1],
            device_id={"cuts": jnp.clip(cut + (1 if up else -1), 0, n_cuts - 1)},
            device_id_type=MESH,
        )

    @pl.when(cut < n_cuts - 1)
    def _():
        edge(True).start()

    @pl.when(cut > 0)
    def _():
        edge(False).start()

    idx[...] = jnp.full(idx.shape, -1, jnp.int32)
    idx[0 : conn.shape[0], 0:cells] = conn[...]
    turned = jnp.transpose(idx[...])[0:cells]
    group[0:cells, :] = turned
    group[cells : cells + 1, :] = halo[...]

    kpad[...] = jnp.zeros(kpad.shape, F32)
    kpad[0 : conn.shape[0], 0 : conn.shape[0]] = cell_matrix[...].astype(F32)
    kmat = kpad[...].astype(BF16)

    place = lax.broadcasted_iota(jnp.int32, (W, W), 0)

    @pl.loop(0, cells + 1)
    def _(c):
        low = group[pl.ds(c, 1), :] & (W - 1)
        onehot[:, pl.ds(pl.multiple_of(c * W, W), W)] = jnp.where(place == low, 1.0, 0.0).astype(BF16)

    ext[half : half + rows, :] = blocks[...]

    @pl.when(me == n_mesh - 1)
    def _():
        win[owned * rows :, :] = jnp.zeros((rows, W), BF16)
        fst[owned * rows :, :] = jnp.zeros((rows, W), BF16)

    @pl.when(me == 0)
    def _():
        ret[...] = jnp.zeros(ret.shape, F32)

    @pl.when(cut > 0)
    def _():
        edge(True).wait_recv()

    @pl.when(cut == 0)
    def _():
        ext[0:half, :] = jnp.zeros((half, nodes), BF16)

    @pl.when(cut < n_cuts - 1)
    def _():
        edge(False).wait_recv()

    @pl.when(cut == n_cuts - 1)
    def _():
        ext[half + rows :, :] = jnp.zeros((half, nodes), BF16)

    pick = (
        lax.broadcasted_iota(jnp.int32, (rows, 2 * rows), 1)
        == lax.broadcasted_iota(jnp.int32, (rows, 2 * rows), 0) + (half + shift[0])
    )
    pick = jnp.where(pick, 1.0, 0.0).astype(BF16)
    for k in range(owned):
        win[k * rows : (k + 1) * rows, :] = dot(pick, ext[:, k * W : (k + 1) * W]).astype(BF16)

    middle, scale = centre[0], 1.0 / half_width[0]

    def gathered(v, c, count):
        found = dot(v[0 : count * rows, :], onehot[:, pl.ds(pl.multiple_of(c * W, W), W)])
        high = jnp.broadcast_to(group[pl.ds(c, 1), :] >> 8, (rows, W))
        total = jnp.zeros((rows, W), F32)
        for k in range(count):
            total = jnp.where(high == k, found[k * rows : (k + 1) * rows], total)
        return total, high

    def spread(value, high, count, split, at):
        kinds = [value]
        if split:
            kinds.append(value - value.astype(BF16).astype(F32))
        for kind, part in enumerate(kinds):
            for k in range(count):
                row = (kind * count + k) * rows
                masked[row : row + rows, at : at + W] = jnp.where(high == k, part, 0.0).astype(BF16)

    def summed(c, width, count, split):
        places = onehot[:, pl.ds(pl.multiple_of(c * W, W), width)]
        height = count * rows
        total = dot(masked[0:height, 0:width], places, NT)
        if split:
            total += dot(masked[height : 2 * height, 0:width], places, NT)
        return total

    def apply_cells(v, at, split):
        def ghost():
            return pltpu.make_async_remote_copy(
                src_ref=ghost_out.at[at],
                dst_ref=v.at[pl.ds(owned * rows, rows)],
                send_sem=ghost_send.at[at],
                recv_sem=ghost_recv.at[at],
                device_id={"mesh": jnp.maximum(me - 1, 0)},
                device_id_type=MESH,
            )

        def back():
            return pltpu.make_async_remote_copy(
                src_ref=acc.at[at, pl.ds(owned * rows, rows)],
                dst_ref=ret.at[at],
                send_sem=ret_send.at[at],
                recv_sem=ret_recv.at[at],
                device_id={"mesh": jnp.minimum(me + 1, n_mesh - 1)},
                device_id_type=MESH,
            )

        ghost_out[at] = gathered(v, cells, owned)[0].astype(BF16)

        @pl.when(me > 0)
        def _():
            ghost().start()

        acc[at] = jnp.zeros(acc.shape[1:], F32)

        @pl.when(me < n_mesh - 1)
        def _():
            ghost().wait_recv()

        @pl.loop(0, cells // UNROLL)
        def _(step):
            for u in range(UNROLL):
                c = step * UNROLL + u
                values, high = gathered(v, c, parts)
                products = dot(values.astype(BF16), kmat, NT) * coef[c]
                spread(products, high, parts, split, u * W)
            acc[at] += summed(step * UNROLL, UNROLL * W, parts, split)

        @pl.when(me < n_mesh - 1)
        def _():
            back().start()

        @pl.when(me > 0)
        def _():
            back().wait_recv()

        high = jnp.broadcast_to(group[cells : cells + 1, :] >> 8, (rows, W))
        spread(ret[at], high, owned, True, 0)
        acc[at, 0 : owned * rows, :] += summed(cells, W, owned, True)

        @pl.when(me > 0)
        def _():
            ghost().wait_send()

        @pl.when(me < n_mesh - 1)
        def _():
            back().wait_send()

    def operated(v, at, k):
        own = slice(k * rows, (k + 1) * rows)
        cols = slice(k * W, (k + 1) * W)
        return (
            acc[at, own, :] / mass[:, cols] + (potential[:, cols] - middle) * v[own, :].astype(F32)
        ) * scale

    apply_cells(win, 0, True)
    for k in range(owned):
        fst[k * rows : (k + 1) * rows, :] = operated(win, 0, k).astype(BF16)
    apply_cells(fst, 1, False)
    partial = jnp.zeros((rows, rows), F32)
    for k in range(owned):
        cols = slice(k * W, (k + 1) * W)
        piece = 2.0 * operated(fst, 1, k) - win[k * rows : (k + 1) * rows, :].astype(F32)
        second[:, cols] = piece
        partial += dot(piece * mass[:, cols], piece, NT, lax.Precision.HIGHEST)
    partial = partial / (nodes * n_mesh)
    grams[pl.ds(me, 1)] = jnp.concatenate([partial, jnp.zeros((rows, rows), F32)], axis=1)[None]

    def share(step):
        return pltpu.make_async_remote_copy(
            src_ref=grams.at[me],
            dst_ref=grams.at[me],
            send_sem=gram_send.at[step],
            recv_sem=gram_recv.at[step],
            device_id={"mesh": lax.rem(me + step, n_mesh)},
            device_id_type=MESH,
        )

    for step in range(1, n_mesh):
        share(step).start()
    for step in range(1, n_mesh):
        share(step).wait_recv()

    work = grams[0]
    for i in range(1, n_mesh):
        work += grams[i]
    line = lax.broadcasted_iota(jnp.int32, (rows, 2 * rows), 0)
    lane = lax.broadcasted_iota(jnp.int32, (rows, 2 * rows), 1)
    work = jnp.where(lane == line + rows, 1.0, work)
    for k in range(rows):
        pivot_row = work[k : k + 1, :]
        column = work[:, k : k + 1]
        pivot = work[k : k + 1, k : k + 1]
        factor = jnp.where(line[:, 0:1] > k, column / pivot, 0.0)
        work = work - factor * pivot_row
    diagonal = jnp.sum(jnp.where(line == lane, work, 0.0), axis=1, keepdims=True)
    inverse = work[:, rows:] / jnp.sqrt(diagonal)
    for k in range(owned):
        cols = slice(k * W, (k + 1) * W)
        out[:, cols] = dot(inverse, second[:, cols], NN, lax.Precision.HIGHEST)

    for step in range(1, n_mesh):
        share(step).wait_send()

    @pl.when(cut < n_cuts - 1)
    def _():
        edge(True).wait_send()

    @pl.when(cut > 0)
    def _():
        edge(False).wait_send()


def body(
    blocks, boundary_shift, centre, half_width, cell_matrix, cell_coef, connectivity, halo_list,
    mass, potential,
):
    n_cuts, n_mesh = lax.axis_size("cuts"), lax.axis_size("mesh")
    rows, nodes = blocks.shape
    cells = connectivity.shape[1]
    parts = nodes // W + 1
    vmem = pl.BlockSpec(memory_space=pltpu.VMEM)
    smem = pl.BlockSpec(memory_space=pltpu.SMEM)
    dma = pltpu.SemaphoreType.DMA
    return pl.pallas_call(
        functools.partial(kernel, n_cuts, n_mesh),
        out_shape=jax.ShapeDtypeStruct((rows, nodes), F32),
        in_specs=[vmem, smem, smem, smem, vmem, smem, vmem, vmem, vmem, vmem],
        out_specs=vmem,
        scratch_shapes=[
            pltpu.VMEM((2 * rows, nodes), BF16),
            pltpu.VMEM((parts * rows, W), BF16),
            pltpu.VMEM((parts * rows, W), BF16),
            pltpu.VMEM((W, (cells + 1) * W), BF16),
            pltpu.VMEM((W, 128), jnp.int32),
            pltpu.VMEM((cells + 8, W), jnp.int32),
            pltpu.VMEM((W, W), F32),
            pltpu.VMEM((2, parts * rows, W), F32),
            pltpu.VMEM((2 * parts * rows, UNROLL * W), BF16),
            pltpu.VMEM((2, rows, W), BF16),
            pltpu.VMEM((2, rows, W), F32),
            pltpu.VMEM((rows, nodes), F32),
            pltpu.VMEM((n_mesh, rows, 2 * rows), F32),
            dma((2,)), dma((2,)), dma((2,)), dma((2,)), dma((2,)), dma((2,)),
            dma((n_mesh,)), dma((n_mesh,)),
        ],
        compiler_params=pltpu.CompilerParams(
            collective_id=0, has_side_effects=True, vmem_limit_bytes=48 * 1024 * 1024
        ),
    )(
        blocks, boundary_shift, centre, half_width, cell_matrix, cell_coef, connectivity,
        halo_list.reshape(1, -1), mass.reshape(1, -1), potential.reshape(1, -1),
    )


def solution(mesh):
    return jax.shard_map(
        body,
        mesh=mesh,
        in_specs=(
            P(("job", "cuts"), "mesh"),
            P(("job", "cuts")),
            P(("job", "cuts")),
            P(("job", "cuts")),
            P(),
            P(("job", "mesh")),
            P(None, ("job", "mesh")),
            P(("job", "mesh")),
            P(("job", "mesh")),
            P(("job", "mesh")),
        ),
        out_specs=P(("job", "cuts"), "mesh"),
        check_vma=False,
    )
```

time: 215 us -> 75.3 us (0.35)
  the two profiles are of different devices: /device:TPU:2 before, /device:TPU:1 now
where the time goes in v1:
time: 75.3 us; the launch traced here: 74 us
  Pallas kernels  69.2 us (92%)
  local copies, waits for them, and re-layouts  2.77 us (4%)
  between operations  2.06 us (3%)
    pallas_call x1, Pallas kernels, body(): pl.pallas_call(functools.partial(kernel, n_cuts, n_mesh), out_shape=jax.S...  69.2 us
    unnamed x14, local copies, waits for them, and re-layouts  2.77 us

profile of v1, /device:TPU:1, one launch (start us, length us, event | category | flops | bytes accessed | tf_op | source)
XLA Modules:
  0.0 74.0 jit_solution(6266553687969245118)
XLA Ops:
  0.0 0.0 copy-start.1
  2.0 0.0 copy-start.2
  2.0 0.0 copy-start.3
  2.0 0.0 copy-start.4
  2.0 0.0 copy-start.5
  2.0 0.9 %copy.11.conn = s32[216,32]{1,0:T(8,128)S(1)} copy(s32[216,32]{0,1:T(8,128)} %param.16) | data formatting | bytes 55296 | tf_op args[6]
  2.9 0.0 copy-done.1
  2.9 0.0 copy-done.2
  2.9 0.0 copy-done.3
  2.9 0.0 copy-done.4
  2.9 0.0 copy-done.5
  2.9 0.0 copy-start
  3.0 1.0 %copy-done = bf16[64,3072]{1,0:T(8,128)(2,1)S(1)} copy-done((bf16[64,3072]{1,0:T(8,128)(2,1)S(1)}, bf16[64,3072]{1,0:T(8,128)(2,1)}, u32[]{:S(2)}) %copy-start) | copy-done | bytes 393240
  3.9 69.2 %shard_map.100 = f32[64,3072]{1,0:T(8,128)S(1)} custom-call(bf16[64,3072]{1,0:T(8,128)(2,1)S(1)} %copy-done, s32[1]{0:T(128)S(6)} %copy.13.shift, f32[1]{0:T(128)S(6)} %copy.14.centre, f32[1]{0:T(128)S(6)} %copy.15.half_width, bf16[216,216]{1,0:T(8,128)(2,1)S(1)} %copy-done.1, f32[32]{0:T(128)S(1)} %copy-done.5, s32[216,32]{1,0:T(8,128)S(1)} %copy.11.conn, ...), custom_call_target="tpu_custom_call" | custom-call | tf_op jit(solution)/shard_map/pallas_call | solution.py:287
  73.2 0.9 %copy.16 = f32[64,3072]{1,0:T(8,128)} copy(f32[64,3072]{1,0:T(8,128)S(1)} %shard_map.100) | data formatting | bytes 1572864
Async XLA Ops:
  0.0 2.9 %copy-start.1 = (bf16[216,216]{1,0:T(8,128)(2,1)S(1)}, bf16[216,216]{1,0:T(8,128)(2,1)}, u32[]{:S(2)}) copy-start(bf16[216,216]{1,0:T(8,128)(2,1)} %cell_matrix.1) | copy-start | bytes 279940
  2.0 0.9 %copy-start.2 = (f32[3072]{0:T(1024)S(1)}, f32[3072]{0:T(1024)}, u32[]{:S(2)}) copy-start(f32[3072]{0:T(1024)} %param.18) | copy-start | bytes 36868
  2.0 0.9 %copy-start.3 = (f32[3072]{0:T(1024)S(1)}, f32[3072]{0:T(1024)}, u32[]{:S(2)}) copy-start(f32[3072]{0:T(1024)} %param.19) | copy-start | bytes 36868
  2.0 0.9 %copy-start.4 = (s32[256]{0:T(256)S(1)}, s32[256]{0:T(256)}, u32[]{:S(2)}) copy-start(s32[256]{0:T(256)} %param.17) | copy-start | bytes 3076
  2.0 0.9 %copy-start.5 = (f32[32]{0:T(128)S(1)}, f32[32]{0:T(128)}, u32[]{:S(2)}) copy-start(f32[32]{0:T(128)} %coef.1) | copy-start | bytes 388
  2.9 1.0 %copy-start = (bf16[64,3072]{1,0:T(8,128)(2,1)S(1)}, bf16[64,3072]{1,0:T(8,128)(2,1)}, u32[]{:S(2)}) copy-start(bf16[64,3072]{1,0:T(8,128)(2,1)} %blocks.1) | copy-start | bytes 1179652

commit v2 on v1

--- a/solution.py
+++ b/solution.py
@@ -9,7 +9,8 @@
 MESH = pl.DeviceIdType.MESH
 F32, BF16 = jnp.float32, jnp.bfloat16
 W = 256
-UNROLL = 4
+UNROLL = 8
+PIVOTS = 4
 NT = (((1,), (1,)), ((), ()))
 NN = (((1,), (0,)), ((), ()))
 
@@ -22,14 +23,13 @@
     n_cuts, n_mesh,
     blocks, shift, centre, half_width, cell_matrix, coef, conn, halo, mass, potential,
     out,
-    ext, win, fst, onehot, idx, group, kpad, acc, masked, ghost_out, ret, second, grams,
+    ext, win, fst, onehot, idx, group, kpad, acc, masked, vals, prods, ghost_out, back_out, ret, second, grams,
     cut_send, cut_recv, ghost_send, ghost_recv, ret_send, ret_recv, gram_send, gram_recv,
 ):
     rows, nodes = blocks.shape
     half = rows // 2
     cells = conn.shape[1]
     owned = nodes // W
-    parts = owned + 1
     cut, me = lax.axis_index("cuts"), lax.axis_index("mesh")
 
     barrier = pltpu.get_barrier_semaphore()
@@ -75,7 +75,7 @@
 
     kpad[...] = jnp.zeros(kpad.shape, F32)
     kpad[0 : conn.shape[0], 0 : conn.shape[0]] = cell_matrix[...].astype(F32)
-    kmat = kpad[...].astype(BF16)
+    kmat = jnp.transpose(kpad[...]).astype(BF16)
 
     place = lax.broadcasted_iota(jnp.int32, (W, W), 0)
 
@@ -121,29 +121,36 @@
 
     middle, scale = centre[0], 1.0 / half_width[0]
 
-    def gathered(v, c, count):
-        found = dot(v[0 : count * rows, :], onehot[:, pl.ds(pl.multiple_of(c * W, W), W)])
-        high = jnp.broadcast_to(group[pl.ds(c, 1), :] >> 8, (rows, W))
+    def tile(c, width=W):
+        return onehot[:, pl.ds(pl.multiple_of(c * W, W), width)]
+
+    def high_of(c):
+        return jnp.broadcast_to(group[pl.ds(c, 1), :] >> 8, (rows, W))
+
+    def gathered(v, c):
+        found = dot(v[0 : owned * rows, :], tile(c))
+        high = high_of(c)
         total = jnp.zeros((rows, W), F32)
-        for k in range(count):
+        for k in range(owned):
             total = jnp.where(high == k, found[k * rows : (k + 1) * rows], total)
-        return total, high
-
-    def spread(value, high, count, split, at):
-        kinds = [value]
+        return total.astype(BF16)
+
+    def kinds_of(value, split):
+        if not split:
+            return [value]
+        return [value, value - value.astype(BF16).astype(F32)]
+
+    def spread(value, high, split, at):
+        for kind, part in enumerate(kinds_of(value, split)):
+            for k in range(owned):
+                row = (kind * owned + k) * rows
+                masked[row : row + rows, at : at + W] = jnp.where(high == k, part, 0.0).astype(BF16)
+
+    def summed(c, width, split):
+        height = owned * rows
+        total = dot(masked[0:height, 0:width], tile(c, width), NT)
         if split:
-            kinds.append(value - value.astype(BF16).astype(F32))
-        for kind, part in enumerate(kinds):
-            for k in range(count):
-                row = (kind * count + k) * rows
-                masked[row : row + rows, at : at + W] = jnp.where(high == k, part, 0.0).astype(BF16)
-
-    def summed(c, width, count, split):
-        places = onehot[:, pl.ds(pl.multiple_of(c * W, W), width)]
-        height = count * rows
-        total = dot(masked[0:height, 0:width], places, NT)
-        if split:
-            total += dot(masked[height : 2 * height, 0:width], places, NT)
+            total += dot(masked[height : 2 * height, 0:width], tile(c, width), NT)
         return total
 
     def apply_cells(v, at, split):
@@ -159,7 +166,7 @@
 
         def back():
             return pltpu.make_async_remote_copy(
-                src_ref=acc.at[at, pl.ds(owned * rows, rows)],
+                src_ref=back_out.at[at],
                 dst_ref=ret.at[at],
                 send_sem=ret_send.at[at],
                 recv_sem=ret_recv.at[at],
@@ -167,38 +174,68 @@
                 device_id_type=MESH,
             )
 
-        ghost_out[at] = gathered(v, cells, owned)[0].astype(BF16)
+        ghost_out[at] = gathered(v, cells)
 
         @pl.when(me > 0)
         def _():
             ghost().start()
-
-        acc[at] = jnp.zeros(acc.shape[1:], F32)
-
-        @pl.when(me < n_mesh - 1)
-        def _():
-            ghost().wait_recv()
 
         @pl.loop(0, cells // UNROLL)
         def _(step):
             for u in range(UNROLL):
                 c = step * UNROLL + u
-                values, high = gathered(v, c, parts)
-                products = dot(values.astype(BF16), kmat, NT) * coef[c]
-                spread(products, high, parts, split, u * W)
-            acc[at] += summed(step * UNROLL, UNROLL * W, parts, split)
+                vals[pl.ds(pl.multiple_of(c * rows, rows), rows), :] = gathered(v, c)
+
+        acc[...] = jnp.zeros(acc.shape, F32)
+        back_out[at] = jnp.zeros((rows, W), F32)
 
         @pl.when(me < n_mesh - 1)
         def _():
+            ghost().wait_recv()
+
+        @pl.loop(0, cells // UNROLL)
+        def _(step):
+            base = pl.multiple_of(step * (UNROLL * rows), UNROLL * rows)
+            outer = v[owned * rows :, :]
+            full = []
+            for u in range(UNROLL):
+                c = step * UNROLL + u
+                found = dot(outer, tile(c))
+                own = vals[pl.ds(pl.multiple_of(c * rows, rows), rows), :].astype(F32)
+                full.append(jnp.where(high_of(c) == owned, found, own).astype(BF16))
+            results = dot(jnp.concatenate(full, axis=0), kmat)
+            sums = jnp.zeros((rows, W), F32)
+            lefts = []
+            for u in range(UNROLL):
+                c = step * UNROLL + u
+                product = results[u * rows : (u + 1) * rows] * coef[c]
+                prods[pl.ds(pl.multiple_of(c * rows, rows), rows), :] = product
+                edge_part = jnp.where(high_of(c) == owned, product, 0.0)
+                lefts.append(
+                    jnp.concatenate([p.astype(BF16) for p in kinds_of(edge_part, split)], axis=0)
+                )
+            both = dot(jnp.concatenate(lefts, axis=1), tile(step * UNROLL, UNROLL * W), NT)
+            sums = both[0:rows] + both[rows:] if split else both
+            back_out[at] += sums
+
+        @pl.when(me < n_mesh - 1)
+        def _():
             back().start()
 
+        @pl.loop(0, cells // UNROLL)
+        def _(step):
+            for u in range(UNROLL):
+                c = step * UNROLL + u
+                product = prods[pl.ds(pl.multiple_of(c * rows, rows), rows), :]
+                spread(product, high_of(c), split, u * W)
+            acc[...] += summed(step * UNROLL, UNROLL * W, split)
+
         @pl.when(me > 0)
         def _():
             back().wait_recv()
 
-        high = jnp.broadcast_to(group[cells : cells + 1, :] >> 8, (rows, W))
-        spread(ret[at], high, owned, True, 0)
-        acc[at, 0 : owned * rows, :] += summed(cells, W, owned, True)
+        spread(ret[at], high_of(cells), True, 0)
+        acc[...] += summed(cells, W, True)
 
         @pl.when(me > 0)
         def _():
@@ -212,7 +249,7 @@
         own = slice(k * rows, (k + 1) * rows)
         cols = slice(k * W, (k + 1) * W)
         return (
-            acc[at, own, :] / mass[:, cols] + (potential[:, cols] - middle) * v[own, :].astype(F32)
+            acc[own, :] / mass[:, cols] + (potential[:, cols] - middle) * v[own, :].astype(F32)
         ) * scale
 
     apply_cells(win, 0, True)
@@ -249,17 +286,29 @@
     line = lax.broadcasted_iota(jnp.int32, (rows, 2 * rows), 0)
     lane = lax.broadcasted_iota(jnp.int32, (rows, 2 * rows), 1)
     work = jnp.where(lane == line + rows, 1.0, work)
-    for k in range(rows):
-        pivot_row = work[k : k + 1, :]
-        column = work[:, k : k + 1]
-        pivot = work[k : k + 1, k : k + 1]
-        factor = jnp.where(line[:, 0:1] > k, column / pivot, 0.0)
-        work = work - factor * pivot_row
+    for first in range(0, rows, PIVOTS):
+        columns = [
+            jnp.broadcast_to(work[:, first + j : first + j + 1], work.shape) for j in range(PIVOTS)
+        ]
+        lines = [work[first + j : first + j + 1, :] for j in range(PIVOTS)]
+        for j in range(PIVOTS):
+            at = first + j
+            inverse_pivot = 1.0 / columns[j][at : at + 1, :]
+            scaled = lines[j] * inverse_pivot
+            for i in range(j + 1, PIVOTS):
+                entry = columns[j][first + i : first + i + 1, :]
+                columns[i] = columns[i] - columns[j] * (entry * inverse_pivot)
+                lines[i] = lines[i] - entry * scaled
+            work = work - jnp.where(line > at, columns[j], 0.0) * scaled
     diagonal = jnp.sum(jnp.where(line == lane, work, 0.0), axis=1, keepdims=True)
     inverse = work[:, rows:] / jnp.sqrt(diagonal)
+    rough = inverse.astype(BF16).astype(F32)
+    left = jnp.concatenate([rough, rough, inverse - rough], axis=1).astype(BF16)
     for k in range(owned):
         cols = slice(k * W, (k + 1) * W)
-        out[:, cols] = dot(inverse, second[:, cols], NN, lax.Precision.HIGHEST)
+        upper = second[:, cols].astype(BF16)
+        rest = (second[:, cols] - upper.astype(F32)).astype(BF16)
+        out[:, cols] = dot(left, jnp.concatenate([upper, rest, upper], axis=0))
 
     for step in range(1, n_mesh):
         share(step).wait_send()
@@ -297,9 +346,12 @@
             pltpu.VMEM((W, 128), jnp.int32),
             pltpu.VMEM((cells + 8, W), jnp.int32),
             pltpu.VMEM((W, W), F32),
-            pltpu.VMEM((2, parts * rows, W), F32),
-            pltpu.VMEM((2 * parts * rows, UNROLL * W), BF16),
+            pltpu.VMEM(((parts - 1) * rows, W), F32),
+            pltpu.VMEM((2 * (parts - 1) * rows, UNROLL * W), BF16),
+            pltpu.VMEM((cells * rows, W), BF16),
+            pltpu.VMEM((cells * rows, W), F32),
             pltpu.VMEM((2, rows, W), BF16),
+            pltpu.VMEM((2, rows, W), F32),
             pltpu.VMEM((2, rows, W), F32),
             pltpu.VMEM((rows, nodes), F32),
             pltpu.VMEM((n_mesh, rows, 2 * rows), F32),

time: 75.3 us -> 49.2 us (0.65); the launches traced: 74 us -> 49 us
  Pallas kernels: 69.2 us -> 44.1 us
    pallas_call x1, Pallas kernels: 69.2 us -> 44.1 us  [body(): pl.pallas_call(functools.partial(kernel, n_cuts, n_mesh), out_shape=jax.S...]
where the time goes in v2:
time: 49.2 us; the launch traced here: 49 us
  Pallas kernels  44.1 us (90%)
  local copies, waits for them, and re-layouts  2.77 us (6%)
  between operations  2.06 us (4%)
    pallas_call x1, Pallas kernels, body(): pl.pallas_call(functools.partial(kernel, n_cuts, n_mesh), out_shape=jax.S...  44.1 us
    unnamed x14, local copies, waits for them, and re-layouts  2.77 us

profile of v2, /device:TPU:1, one launch (start us, length us, event | category | flops | bytes accessed | tf_op | source)
XLA Modules:
  0.0 49.0 jit_solution(17011850694048438172)
XLA Ops:
  0.0 0.0 copy-start.1
  2.0 0.0 copy-start.2
  2.0 0.0 copy-start.3
  2.0 0.0 copy-start.4
  2.0 0.0 copy-start.5
  2.0 0.9 %copy.11.conn = s32[216,32]{1,0:T(8,128)S(1)} copy(s32[216,32]{0,1:T(8,128)} %param.16) | data formatting | bytes 55296 | tf_op args[6]
  2.9 0.0 copy-done.1
  2.9 0.0 copy-done.2
  2.9 0.0 copy-done.3
  2.9 0.0 copy-done.4
  2.9 0.0 copy-done.5
  2.9 0.0 copy-start
  3.0 1.0 %copy-done = bf16[64,3072]{1,0:T(8,128)(2,1)S(1)} copy-done((bf16[64,3072]{1,0:T(8,128)(2,1)S(1)}, bf16[64,3072]{1,0:T(8,128)(2,1)}, u32[]{:S(2)}) %copy-start) | copy-done | bytes 393240
  3.9 44.1 %shard_map.100 = f32[64,3072]{1,0:T(8,128)S(1)} custom-call(bf16[64,3072]{1,0:T(8,128)(2,1)S(1)} %copy-done, s32[1]{0:T(128)S(6)} %copy.13.shift, f32[1]{0:T(128)S(6)} %copy.14.centre, f32[1]{0:T(128)S(6)} %copy.15.half_width, bf16[216,216]{1,0:T(8,128)(2,1)S(1)} %copy-done.1, f32[32]{0:T(128)S(1)} %copy-done.5, s32[216,32]{1,0:T(8,128)S(1)} %copy.11.conn, ...), custom_call_target="tpu_custom_call" | custom-call | tf_op jit(solution)/shard_map/pallas_call | solution.py:336
  48.1 0.9 %copy.16 = f32[64,3072]{1,0:T(8,128)} copy(f32[64,3072]{1,0:T(8,128)S(1)} %shard_map.100) | data formatting | bytes 1572864
Async XLA Ops:
  0.0 2.9 %copy-start.1 = (bf16[216,216]{1,0:T(8,128)(2,1)S(1)}, bf16[216,216]{1,0:T(8,128)(2,1)}, u32[]{:S(2)}) copy-start(bf16[216,216]{1,0:T(8,128)(2,1)} %cell_matrix.1) | copy-start | bytes 279940
  2.0 0.9 %copy-start.2 = (f32[3072]{0:T(1024)S(1)}, f32[3072]{0:T(1024)}, u32[]{:S(2)}) copy-start(f32[3072]{0:T(1024)} %param.18) | copy-start | bytes 36868
  2.0 0.9 %copy-start.3 = (f32[3072]{0:T(1024)S(1)}, f32[3072]{0:T(1024)}, u32[]{:S(2)}) copy-start(f32[3072]{0:T(1024)} %param.19) | copy-start | bytes 36868
  2.0 0.9 %copy-start.4 = (s32[256]{0:T(256)S(1)}, s32[256]{0:T(256)}, u32[]{:S(2)}) copy-start(s32[256]{0:T(256)} %param.17) | copy-start | bytes 3076
  2.0 0.9 %copy-start.5 = (f32[32]{0:T(128)S(1)}, f32[32]{0:T(128)}, u32[]{:S(2)}) copy-start(f32[32]{0:T(128)} %coef.1) | copy-start | bytes 388
  2.9 1.0 %copy-start = (bf16[64,3072]{1,0:T(8,128)(2,1)S(1)}, bf16[64,3072]{1,0:T(8,128)(2,1)}, u32[]{:S(2)}) copy-start(bf16[64,3072]{1,0:T(8,128)(2,1)} %blocks.1) | copy-start | bytes 1179652

commit v3 on v2

--- a/solution.py
+++ b/solution.py
@@ -9,8 +9,8 @@
 MESH = pl.DeviceIdType.MESH
 F32, BF16 = jnp.float32, jnp.bfloat16
 W = 256
-UNROLL = 8
-PIVOTS = 4
+UNROLL = 16
+PIVOTS = 8
 NT = (((1,), (1,)), ((), ()))
 NN = (((1,), (0,)), ((), ()))
 

time: 49.2 us -> 46.3 us (0.941)
  Pallas kernels: 44.1 us -> 41.2 us
    pallas_call x1, Pallas kernels: 44.1 us -> 41.2 us  [body(): pl.pallas_call(functools.partial(kernel, n_cuts, n_mesh), out_shape=jax.S...]
where the time goes in v3:
time: 46.3 us; the launch traced here: 46.1 us
  Pallas kernels  41.2 us (89%)
  local copies, waits for them, and re-layouts  2.77 us (6%)
  between operations  2.06 us (4%)
    pallas_call x1, Pallas kernels, body(): pl.pallas_call(functools.partial(kernel, n_cuts, n_mesh), out_shape=jax.S...  41.2 us
    unnamed x14, local copies, waits for them, and re-layouts  2.77 us

profile of v3, /device:TPU:1, one launch (start us, length us, event | category | flops | bytes accessed | tf_op | source)
XLA Modules:
  0.0 46.1 jit_solution(564314262666567379)
XLA Ops:
  0.0 0.0 copy-start.1
  2.0 0.0 copy-start.2
  2.0 0.0 copy-start.3
  2.0 0.0 copy-start.4
  2.0 0.0 copy-start.5
  2.0 0.9 %copy.11.conn = s32[216,32]{1,0:T(8,128)S(1)} copy(s32[216,32]{0,1:T(8,128)} %param.16) | data formatting | bytes 55296 | tf_op args[6]
  2.9 0.0 copy-done.1
  2.9 0.0 copy-done.2
  2.9 0.0 copy-done.3
  2.9 0.0 copy-done.4
  2.9 0.0 copy-done.5
  2.9 0.0 copy-start
  3.0 1.0 %copy-done = bf16[64,3072]{1,0:T(8,128)(2,1)S(1)} copy-done((bf16[64,3072]{1,0:T(8,128)(2,1)S(1)}, bf16[64,3072]{1,0:T(8,128)(2,1)}, u32[]{:S(2)}) %copy-start) | copy-done | bytes 393240
  3.9 41.2 %shard_map.100 = f32[64,3072]{1,0:T(8,128)S(1)} custom-call(bf16[64,3072]{1,0:T(8,128)(2,1)S(1)} %copy-done, s32[1]{0:T(128)S(6)} %copy.13.shift, f32[1]{0:T(128)S(6)} %copy.14.centre, f32[1]{0:T(128)S(6)} %copy.15.half_width, bf16[216,216]{1,0:T(8,128)(2,1)S(1)} %copy-done.1, f32[32]{0:T(128)S(1)} %copy-done.5, s32[216,32]{1,0:T(8,128)S(1)} %copy.11.conn, ...), custom_call_target="tpu_custom_call" | custom-call | tf_op jit(solution)/shard_map/pallas_call | solution.py:336
  45.2 0.9 %copy.16 = f32[64,3072]{1,0:T(8,128)} copy(f32[64,3072]{1,0:T(8,128)S(1)} %shard_map.100) | data formatting | bytes 1572864
Async XLA Ops:
  0.0 2.9 %copy-start.1 = (bf16[216,216]{1,0:T(8,128)(2,1)S(1)}, bf16[216,216]{1,0:T(8,128)(2,1)}, u32[]{:S(2)}) copy-start(bf16[216,216]{1,0:T(8,128)(2,1)} %cell_matrix.1) | copy-start | bytes 279940
  2.0 0.9 %copy-start.2 = (f32[3072]{0:T(1024)S(1)}, f32[3072]{0:T(1024)}, u32[]{:S(2)}) copy-start(f32[3072]{0:T(1024)} %param.18) | copy-start | bytes 36868
  2.0 0.9 %copy-start.3 = (f32[3072]{0:T(1024)S(1)}, f32[3072]{0:T(1024)}, u32[]{:S(2)}) copy-start(f32[3072]{0:T(1024)} %param.19) | copy-start | bytes 36868
  2.0 0.9 %copy-start.4 = (s32[256]{0:T(256)S(1)}, s32[256]{0:T(256)}, u32[]{:S(2)}) copy-start(s32[256]{0:T(256)} %param.17) | copy-start | bytes 3076
  2.0 0.9 %copy-start.5 = (f32[32]{0:T(128)S(1)}, f32[32]{0:T(128)}, u32[]{:S(2)}) copy-start(f32[32]{0:T(128)} %coef.1) | copy-start | bytes 388
  2.9 1.0 %copy-start = (bf16[64,3072]{1,0:T(8,128)(2,1)S(1)}, bf16[64,3072]{1,0:T(8,128)(2,1)}, u32[]{:S(2)}) copy-start(bf16[64,3072]{1,0:T(8,128)(2,1)} %blocks.1) | copy-start | bytes 1179652
